TPU v7x, 256 devices: a whole 4x4x8 slice. The times are simulated.
256 devices in a mesh: segment: 16 (over z_lo, y), expert: 16 (over x, z_hi, core).
Axes of the slice: x: 4, y: 4, z: 8 (z_hi: 2, z_lo: 4; z = z_hi * 4 + z_lo), core: 2. Of those that a mesh axis runs over, the one named last changes fastest.
Arguments:
- rising_acts: bfloat16 [16, 2048, 3584], P('segment', 'expert'), may hold values from -6 to 6
- falling_acts: bfloat16 [16, 2048, 3584], P('segment', 'expert'), may hold values from -6 to 6
- norm_gain: float32 [16, 3584], P('segment'), may hold values from 0.5 to 1.5
- router_weight: float32 [16, 3584, 4], P('segment'), may hold values from -0.1875 to 0.1875
- gate_weight: bfloat16 [16, 3584, 4096], P('segment', None, 'expert'), may hold values from -0.09375 to 0.09375
- up_weight: bfloat16 [16, 3584, 4096], P('segment', None, 'expert'), may hold values from -0.09375 to 0.09375
- down_weight: bfloat16 [16, 4096, 3584], P('segment', 'expert'), may hold values from -0.1875 to 0.1875
- rising_ids: int32 [16, 64, 2], P('segment', 'expert'), may hold values from 0 to 3, all different within a row; in each aligned block of 4 rows (0 to 3, 4 to 7, ..., all dimensions but the last counted through in order) at most 2 rows name the same one
- falling_ids: int32 [16, 64, 2], P('segment', 'expert'), may hold values from 0 to 3, all different within a row; in each aligned block of 4 rows (0 to 3, 4 to 7, ..., all dimensions but the last counted through in order) at most 2 rows name the same one
Outputs:
- rising_next: bfloat16 [16, 2048, 3584], P('segment', 'expert')
- falling_next: bfloat16 [16, 2048, 3584], P('segment', 'expert')
Inputs may be any that keep to these rules, and one draw needn't show every extreme that they name: `rising_ids`: within the 4 blocks of one index of expert in one section, every expert is named by exactly 2 blocks. `falling_ids`: within the 4 blocks of one index of expert in one section, every expert is named by exactly 2 blocks.
All inputs are finite; a program needn't handle non-finite values.
Results may differ from a plain program's by a relative error of at most 0.009.
Values may be sent and summed in bfloat16 or wider, within the bound.
A program may use at most 128 MiB of HBM per device.

v0:
```python
import jax
import jax.numpy as jnp
from jax import lax
from jax.sharding import PartitionSpec as P

CAP = 2


eps = 1e-06
route_scale = 2.5


def from_behind(value, axis, steps):
    count = lax.axis_size(axis)
    pairs = [(source, (source + steps) % count) for source in range(count)]
    return lax.ppermute(value, axis, pairs)


def pair_levels(stacked):
    stacked = lax.optimization_barrier(
        (stacked[:, 0::2].astype(jnp.float32) + stacked[:, 1::2].astype(jnp.float32)).astype(
            jnp.bfloat16
        )
    )
    return stacked[:, 0].astype(jnp.float32) + stacked[:, 1].astype(jnp.float32)


def moe_layer(acts, route_ids, gain_row, router, gate_slab, up_slab, down_slab):
    devices = lax.axis_size("expert")
    tokens, features = acts.shape
    blocks = route_ids.shape[0]
    block_rows = tokens // blocks
    experts = router.shape[1]
    group_size = devices // experts
    widened = acts.astype(jnp.float32)
    square_mean = jnp.mean(widened * widened, axis=-1, keepdims=True)
    normed = (widened * lax.rsqrt(square_mean + eps) * gain_row).astype(jnp.bfloat16)
    scores = jax.nn.sigmoid(
        jnp.dot(normed.astype(jnp.float32), router, precision=lax.Precision.HIGHEST)
    )
    chosen_int = jnp.any(
        route_ids[:, :, None] == jnp.arange(experts, dtype=jnp.int32)[None, None, :], axis=1
    ).astype(jnp.int32)
    chosen = chosen_int.astype(jnp.float32)
    weighted = scores.reshape(blocks, block_rows, experts) * chosen[:, None, :]
    gate_share = weighted / jnp.sum(weighted, axis=-1, keepdims=True)
    slot_rank = jnp.cumsum(chosen_int, axis=0) - chosen_int
    slot_ids = jnp.arange(CAP, dtype=jnp.int32)
    selector = (
        chosen_int[:, :, None] * (slot_rank[:, :, None] == slot_ids).astype(jnp.int32)
    ).astype(jnp.float32)
    normed_blocks = normed.reshape(blocks, block_rows, features)
    picked = jnp.einsum(
        "bec,brd->ecrd",
        selector.astype(jnp.bfloat16),
        normed_blocks,
        preferred_element_type=jnp.float32,
    ).astype(jnp.bfloat16)
    outgoing = jnp.repeat(picked, group_size, axis=0)
    received = lax.all_to_all(outgoing, "expert", split_axis=0, concat_axis=0, tiled=True)
    arrived = received.reshape(devices * CAP * block_rows, features)
    gate_pre = jnp.dot(arrived, gate_slab, preferred_element_type=jnp.float32)
    up_pre = jnp.dot(arrived, up_slab, preferred_element_type=jnp.float32)
    hidden = (jax.nn.silu(gate_pre) * up_pre).astype(jnp.bfloat16)
    partial_value = jnp.dot(hidden, down_slab, preferred_element_type=jnp.float32).astype(
        jnp.bfloat16
    )
    returned = lax.all_to_all(
        partial_value.reshape(devices, CAP, block_rows, features),
        "expert",
        split_axis=0,
        concat_axis=0,
        tiled=True,
    )
    summed = pair_levels(returned.reshape(experts, group_size, CAP, block_rows, features))
    restored = jnp.einsum("bec,ecrd->bred", selector, summed)
    contribution = jnp.sum(gate_share[..., None] * restored, axis=2)
    mixed = widened.reshape(blocks, block_rows, features) + route_scale * contribution
    return mixed.reshape(tokens, features).astype(jnp.bfloat16)


def on_device(
    rising_acts,
    falling_acts,
    norm_gain,
    router_weight,
    gate_weight,
    up_weight,
    down_weight,
    rising_ids,
    falling_ids,
):
    gain_row = norm_gain[0]
    router = router_weight[0]
    gate_slab = gate_weight[0]
    up_slab = up_weight[0]
    down_slab = down_weight[0]
    rising_out = moe_layer(
        rising_acts[0], rising_ids[0], gain_row, router, gate_slab, up_slab, down_slab
    )
    falling_out = moe_layer(
        falling_acts[0], falling_ids[0], gain_row, router, gate_slab, up_slab, down_slab
    )
    rising_next = from_behind(rising_out[None], "segment", 1)
    falling_next = from_behind(falling_out[None], "segment", -1)
    return (rising_next, falling_next)


def solution(mesh):
    return jax.shard_map(
        on_device,
        mesh=mesh,
        in_specs=(
            P("segment", "expert", None),
            P("segment", "expert", None),
            P("segment", None),
            P("segment", None, None),
            P("segment", None, "expert"),
            P("segment", None, "expert"),
            P("segment", "expert", None),
            P("segment", "expert", None),
            P("segment", "expert", None),
        ),
        out_specs=(P("segment", "expert", None), P("segment", "expert", None)),
        check_vma=False,
    )
```

profile of v0, /device:TPU:1, one launch (start us, length us, event | category | flops | bytes accessed | tf_op | source)
XLA Modules:
  0.0 751.4 jit_solution(7630544244803460393)
XLA Ops:
  3.4 2.6 convert.3
  6.1 3.2 convolution_convert_fusion.2
  9.7 3.8 broadcast_in_dim.5
  13.5 12.6 %all-to-all-start.2 = ((bf16[16,2,32,3584]{3,2,1,0:T(8,128)(2,1)}), bf16[16,2,32,3584]{3,2,1,0:T(8,128)(2,1)}, u32[]{:S(2)}, u32[]{:S(2)}) async-start(bf16[16,2,32,3584]{3,2,1,0:T(8,128)(2,1)} %bitcast.114), calls=%async_computation.2 | async-start | bytes 14680064 | tf_op jit(solution)/shard_map/all_to_all | solution.py:60
  27.0 1.8 convolution_convert_fusion.3
  30.4 162.4 %all-to-all-done.2 = bf16[16,2,32,3584]{3,2,1,0:T(8,128)(2,1)} async-done(((bf16[16,2,32,3584]{3,2,1,0:T(8,128)(2,1)}), bf16[16,2,32,3584]{3,2,1,0:T(8,128)(2,1)}, u32[]{:S(2)}, u32[]{:S(2)}) %all-to-all-start.2) | async-done | bytes 7340064 | tf_op jit(solution)/shard_map/all_to_all | solution.py:60
  192.8 5.3 broadcast_in_dim.4
  198.1 6.7 all-to-all-start
  204.8 6.7 fusion.12
  211.5 15.3 %convolution_convert_fusion = bf16[1024,3584]{1,0:T(8,128)(2,1)} fusion(bf16[1,256,3584]{2,1,0:T(8,128)(2,1)S(1)} %copy-done, bf16[1024,3584]{1,0:T(8,128)(2,1)} %bitcast.24, bf16[1,3584,256]{2,1,0:T(8,128)(2,1)} %param.14, f32[1024,256]{1,0:T(8,128)} %fusion.12), kind=kOutput, calls=%fused_computation | convolution fusion | flops 3763339264 | bytes 19398656 | tf_op jit(solution)/shard_map/dot_general | solution.py:65
  226.8 65.9 %all-to-all-done = bf16[16,2,32,3584]{3,2,1,0:T(8,128)(2,1)} async-done(((bf16[16,2,32,3584]{3,2,1,0:T(8,128)(2,1)}), bf16[16,2,32,3584]{3,2,1,0:T(8,128)(2,1)}, u32[]{:S(2)}, u32[]{:S(2)}) %all-to-all-start) | async-done | bytes 7340064 | tf_op jit(solution)/shard_map/all_to_all | solution.py:60
  292.7 5.3 all-to-all-start.3
  298.0 6.7 fusion.14
  304.7 15.3 %convolution_convert_fusion.1 = bf16[1024,3584]{1,0:T(8,128)(2,1)} fusion(bf16[1,256,3584]{2,1,0:T(8,128)(2,1)S(1)} %copy-done, bf16[1024,3584]{1,0:T(8,128)(2,1)} %bitcast.7, bf16[1,3584,256]{2,1,0:T(8,128)(2,1)} %param.14, f32[1024,256]{1,0:T(8,128)} %fusion.14), kind=kOutput, calls=%fused_computation.1 | convolution fusion | flops 3763339264 | bytes 19398656 | tf_op jit(solution)/shard_map/dot_general | solution.py:65
  319.9 130.4 %all-to-all-done.3 = bf16[16,2,32,3584]{3,2,1,0:T(8,128)(2,1)} async-done(((bf16[16,2,32,3584]{3,2,1,0:T(8,128)(2,1)}), bf16[16,2,32,3584]{3,2,1,0:T(8,128)(2,1)}, u32[]{:S(2)}, u32[]{:S(2)}) %all-to-all-start.3) | async-done | bytes 7340064 | tf_op jit(solution)/shard_map/all_to_all | solution.py:68
  450.3 8.6 %all-to-all-start.1 = ((bf16[16,2,32,3584]{3,2,1,0:T(8,128)(2,1)}), bf16[16,2,32,3584]{3,2,1,0:T(8,128)(2,1)}, u32[]{:S(2)}, u32[]{:S(2)}) async-start(bf16[16,2,32,3584]{3,2,1,0:T(8,128)(2,1)} %bitcast.118), calls=%async_computation.1 | async-start | bytes 14680064 | tf_op jit(solution)/shard_map/all_to_all | solution.py:68
  462.0 4.2 add_convert_fusion
  466.7 4.4 fusion
  472.9 91.7 %collective-permute-start.1 = (bf16[1,128,3584]{2,1,0:T(8,128)(2,1)}, bf16[1,128,3584]{2,1,0:T(8,128)(2,1)}, u32[]{:S(2)}, u32[]{:S(2)}) collective-permute-start(bf16[1,128,3584]{2,1,0:T(8,128)(2,1)} %fusion.4), channel_id=1, source_target_pairs={{0,240},{16,0},{32,16},{48,32},{64,48},{80,64},{96,80},{112,96},{1... | collective-permute-start | bytes 2752520 | tf_op jit(solution)/shard_map/ppermute | solution.py:16
  564.7 47.8 %all-to-all-done.1 = bf16[16,2,32,3584]{3,2,1,0:T(8,128)(2,1)} async-done(((bf16[16,2,32,3584]{3,2,1,0:T(8,128)(2,1)}), bf16[16,2,32,3584]{3,2,1,0:T(8,128)(2,1)}, u32[]{:S(2)}, u32[]{:S(2)}) %all-to-all-start.1) | async-done | bytes 7340064 | tf_op jit(solution)/shard_map/all_to_all | solution.py:68
  612.4 4.2 add_convert_fusion.1
  617.2 4.4 fusion.1
  625.4 122.9 %collective-permute-done = bf16[1,128,3584]{2,1,0:T(8,128)(2,1)S(1)} collective-permute-done((bf16[1,128,3584]{2,1,0:T(8,128)(2,1)S(1)}, bf16[1,128,3584]{2,1,0:T(8,128)(2,1)S(1)}, u32[]{:S(2)}, u32[]{:S(2)}) %collective-permute-start) | collective-permute-done | bytes 917536 | tf_op jit(solution)/shard_map/ppermute | solution.py:16
  749.3 2.2 copy.144
  (65 shorter events, 16.4 us)
Async XLA Ops:
  0.6 210.9 %copy-start = (bf16[1,256,3584]{2,1,0:T(8,128)(2,1)S(1)}, bf16[1,256,3584]{2,1,0:T(8,128)(2,1)}, u32[]{:S(2)}) copy-start(bf16[1,256,3584]{2,1,0:T(8,128)(2,1)} %param.15) | copy-start | bytes 5505028
  1.8 4.3 copy-start.4
  13.5 12.6 %copy-start.6 = (s32[1,4,2]{1,2,0:T(2,128)S(1)}, s32[1,4,2]{1,2,0:T(2,128)}, u32[]{:S(2)}) copy-start(s32[1,4,2]{1,2,0:T(2,128)} %param.16) | copy-start | bytes 100
  13.5 12.9 %copy-start.3 = (bf16[1,128,3584]{2,1,0:T(8,128)(2,1)S(1)}, bf16[1,128,3584]{2,1,0:T(8,128)(2,1)}, u32[]{:S(2)}) copy-start(bf16[1,128,3584]{2,1,0:T(8,128)(2,1)} %param.9) | copy-start | bytes 2752516
  13.5 179.3 %all-to-all-start.2 = ((bf16[16,2,32,3584]{3,2,1,0:T(8,128)(2,1)}), bf16[16,2,32,3584]{3,2,1,0:T(8,128)(2,1)}, u32[]{:S(2)}, u32[]{:S(2)}) async-start(bf16[16,2,32,3584]{3,2,1,0:T(8,128)(2,1)} %bitcast.114), calls=%async_computation.2 | async-start | bytes 14680064 | tf_op jit(solution)/shard_map/all_to_all | solution.py:60
  198.1 94.6 %all-to-all-start = ((bf16[16,2,32,3584]{3,2,1,0:T(8,128)(2,1)}), bf16[16,2,32,3584]{3,2,1,0:T(8,128)(2,1)}, u32[]{:S(2)}, u32[]{:S(2)}) async-start(bf16[16,2,32,3584]{3,2,1,0:T(8,128)(2,1)} %bitcast.115), calls=%async_computation | async-start | bytes 14680064 | tf_op jit(solution)/shard_map/all_to_all | solution.py:60
  292.7 157.6 %all-to-all-start.3 = ((bf16[16,2,32,3584]{3,2,1,0:T(8,128)(2,1)}), bf16[16,2,32,3584]{3,2,1,0:T(8,128)(2,1)}, u32[]{:S(2)}, u32[]{:S(2)}) async-start(bf16[16,2,32,3584]{3,2,1,0:T(8,128)(2,1)} %bitcast.119), calls=%async_computation.3 | async-start | bytes 14680064 | tf_op jit(solution)/shard_map/all_to_all | solution.py:68
  450.3 8.8 %copy-start.2 = (bf16[1,128,3584]{2,1,0:T(8,128)(2,1)S(1)}, bf16[1,128,3584]{2,1,0:T(8,128)(2,1)}, u32[]{:S(2)}) copy-start(bf16[1,128,3584]{2,1,0:T(8,128)(2,1)} %param.10) | copy-start | bytes 2752516
  450.3 8.8 %copy-start.5 = (f32[1,3584,4]{1,2,0:T(4,128)S(1)}, f32[1,3584,4]{1,2,0:T(4,128)}, u32[]{:S(2)}) copy-start(f32[1,3584,4]{1,2,0:T(4,128)} %param.12) | copy-start | bytes 172036
  450.3 162.1 %all-to-all-start.1 = ((bf16[16,2,32,3584]{3,2,1,0:T(8,128)(2,1)}), bf16[16,2,32,3584]{3,2,1,0:T(8,128)(2,1)}, u32[]{:S(2)}, u32[]{:S(2)}) async-start(bf16[16,2,32,3584]{3,2,1,0:T(8,128)(2,1)} %bitcast.118), calls=%async_computation.1 | async-start | bytes 14680064 | tf_op jit(solution)/shard_map/all_to_all | solution.py:68
  472.9 152.5 %collective-permute-start.1 = (bf16[1,128,3584]{2,1,0:T(8,128)(2,1)}, bf16[1,128,3584]{2,1,0:T(8,128)(2,1)}, u32[]{:S(2)}, u32[]{:S(2)}) collective-permute-start(bf16[1,128,3584]{2,1,0:T(8,128)(2,1)} %fusion.4), channel_id=1, source_target_pairs={{0,240},{16,0},{32,16},{48,32},{64,48},{80,64},{96,80},{112,96},{1... | collective-permute-start | bytes 2752520 | tf_op jit(solution)/shard_map/ppermute | solution.py:16
  622.2 129.2 %copy-start.1 = (bf16[1,256,3584]{2,1,0:T(8,128)(2,1)S(1)}, bf16[1,256,3584]{2,1,0:T(8,128)(2,1)}, u32[]{:S(2)}) copy-start(bf16[1,256,3584]{2,1,0:T(8,128)(2,1)} %param.15) | copy-start | bytes 5505028
  622.5 125.9 %collective-permute-start = (bf16[1,128,3584]{2,1,0:T(8,128)(2,1)S(1)}, bf16[1,128,3584]{2,1,0:T(8,128)(2,1)S(1)}, u32[]{:S(2)}, u32[]{:S(2)}) collective-permute-start(bf16[1,128,3584]{2,1,0:T(8,128)(2,1)S(1)} %fusion.5), channel_id=1, source_target_pairs={{0,16},{16,32},{32,48},{48,64},{64,80},{80,96},{96,112},{112,128},... | collective-permute-start | bytes 2752520 | tf_op jit(solution)/shard_map/ppermute | solution.py:16
where the time goes:
time: 756 us; the launch traced here: 751 us
  waiting for transfers between devices  531 us (70%)
  starting transfers between devices  126 us (17%)
  matrix products  59.5 us (8%)
  other arithmetic  18 us (2%)
  local copies, waits for them, and re-layouts  15.9 us (2%)
    all_to_all x2, waiting for transfers between devices, moe_layer(): lax.all_to_all(outgoing, 'expert', split_axis=0, concat_axis=0, tiled=True)  228 us
    all_to_all x2, waiting for transfers between devices, moe_layer(): lax.all_to_all(partial_value.reshape(devices, CAP, block_rows, features),...  178 us
    ppermute x2, waiting for transfers between devices, from_behind(): return lax.ppermute(value, axis, pairs)  125 us
    ppermute x2, starting transfers between devices, from_behind(): return lax.ppermute(value, axis, pairs)  93.1 us
    dot_general x2, matrix products, moe_layer(): jnp.dot(hidden, down_slab, preferred_element_type=jnp.float32)  30.5 us
    all_to_all x2, starting transfers between devices, moe_layer(): lax.all_to_all(outgoing, 'expert', split_axis=0, concat_axis=0, tiled=True)  19.3 us
  transfers between devices with their start and end apart: 6, of which 6 were waited for; matrix products, arithmetic and copies ran while one was open for 10% of the time, Pallas kernels for 0%

commit v1 on v0

v1 whole, which is shorter than its diff:
```python
import functools

import jax
import jax.numpy as jnp
from jax import lax
from jax.experimental import pallas as pl
from jax.experimental.pallas import tpu as pltpu
from jax.sharding import PartitionSpec as P

MESH = pl.DeviceIdType.MESH
EPS = 1e-06
ROUTE_SCALE = 2.5
EXPERTS = 4
XN = 4
CHUNKS = 4
BR = 32
LANES = 128
F32 = jnp.float32
BF16 = jnp.bfloat16


def relay_kernel(
    rows,
    features,
    units,
    segments,
    rise_hbm,
    fall_hbm,
    gain_ref,
    router_ref,
    gate_hbm,
    up_hbm,
    down_hbm,
    ids_hbm,
    rise_out,
    fall_out,
    acts,
    gate_w,
    up_w,
    down_w,
    ids_own,
    ids_land,
    ids_far,
    picker,
    mixer,
    mixer_rest,
    normed,
    far_normed,
    sending,
    arrived,
    hidden,
    core_sum,
    returned,
    z_out,
    z_in,
    finished,
    scores,
    act_sem,
    w_sem,
    dw_sem,
    ids_sem,
    ids_ss,
    ids_rs,
    zf_ss,
    zf_rs,
    xf_ss,
    xf_rs,
    df_ss,
    df_rs,
    dp_ss,
    dp_rs,
    xr_ss,
    xr_rs,
    zr_ss,
    zr_rs,
    y_ss,
    y_rs,
):
    width = features // CHUNKS
    pick_rows = 2 * BR
    half = XN * pick_rows
    blocks = rows // BR
    tiles = width // LANES

    seg = lax.axis_index("segment")
    me = lax.axis_index("expert")
    x = me // 4
    core = lax.rem(me, 2)
    z_hi = lax.rem(me // 2, 2)
    z_mate = me + 2 - 4 * z_hi
    core_mate = me + 1 - 2 * core
    seg_up = lax.rem(seg + 1, segments)
    seg_down = lax.rem(seg + segments - 1, segments)
    own_half = pl.multiple_of(core * half, half)
    mate_half = pl.multiple_of((1 - core) * half, half)

    def x_at(i):
        return lax.rem(x + i, XN)

    def x_device(i):
        return me + 4 * (x_at(i) - x)

    def z_forward(mb, k):
        return pltpu.make_async_remote_copy(
            src_ref=normed.at[mb, k],
            dst_ref=far_normed.at[mb, k],
            send_sem=zf_ss.at[mb, k],
            recv_sem=zf_rs.at[mb, k],
            device_id=(seg, z_mate),
            device_id_type=MESH,
        )

    def x_forward(s, k, i):
        return pltpu.make_async_remote_copy(
            src_ref=sending.at[s, k, pl.ds(pl.multiple_of(x_at(i) * pick_rows, pick_rows), pick_rows)],
            dst_ref=arrived.at[s, k, pl.ds(pl.multiple_of(own_half + x * pick_rows, pick_rows), pick_rows)],
            send_sem=xf_ss.at[s, k, i - 1],
            recv_sem=xf_rs.at[s, k, i - 1],
            device_id=(seg, x_device(i)),
            device_id_type=MESH,
        )

    def core_forward(s, k):
        return pltpu.make_async_remote_copy(
            src_ref=arrived.at[s, k, pl.ds(own_half, half)],
            dst_ref=arrived.at[s, k, pl.ds(own_half, half)],
            send_sem=df_ss.at[s, k],
            recv_sem=df_rs.at[s, k],
            device_id=(seg, core_mate),
            device_id_type=MESH,
        )

    def core_part(s, k):
        return pltpu.make_async_remote_copy(
            src_ref=arrived.at[s, k, pl.ds(mate_half, half)],
            dst_ref=core_sum.at[s, k],
            send_sem=dp_ss.at[s, k],
            recv_sem=dp_rs.at[s, k],
            device_id=(seg, core_mate),
            device_id_type=MESH,
        )

    def x_return(s, k, i):
        return pltpu.make_async_remote_copy(
            src_ref=arrived.at[s, k, pl.ds(pl.multiple_of(own_half + x_at(i) * pick_rows, pick_rows), pick_rows)],
            dst_ref=returned.at[s, k, pl.ds(pl.multiple_of(x * pick_rows, pick_rows), pick_rows)],
            send_sem=xr_ss.at[s, k, i - 1],
            recv_sem=xr_rs.at[s, k, i - 1],
            device_id=(seg, x_device(i)),
            device_id_type=MESH,
        )

    def z_return(mb, k):
        return pltpu.make_async_remote_copy(
            src_ref=z_out.at[mb, k],
            dst_ref=z_in.at[mb, k],
            send_sem=zr_ss.at[mb, k],
            recv_sem=zr_rs.at[mb, k],
            device_id=(seg, z_mate),
            device_id_type=MESH,
        )

    def shift(mb, k):
        out = rise_out if mb == 0 else fall_out
        return pltpu.make_async_remote_copy(
            src_ref=finished.at[mb, k],
            dst_ref=out.at[0, :, pl.ds(k * width, width)],
            send_sem=y_ss.at[mb, k],
            recv_sem=y_rs.at[mb, k],
            device_id=(seg_up if mb == 0 else seg_down, me),
            device_id_type=MESH,
        )

    ids_exchange = pltpu.make_async_remote_copy(
        src_ref=ids_hbm,
        dst_ref=ids_land,
        send_sem=ids_ss,
        recv_sem=ids_rs,
        device_id=(seg, z_mate),
        device_id_type=MESH,
    )

    def normalize(mb):
        @pl.loop(0, blocks)
        def _(b):
            at = pl.ds(pl.multiple_of(b * BR, BR), BR)
            value = acts[mb, at, :].astype(F32)
            scale = lax.rsqrt(jnp.mean(value * value, axis=-1, keepdims=True) + EPS)
            for k in range(CHUNKS):
                cut = slice(k * width, (k + 1) * width)
                normed[mb, k, at, :] = (value[:, cut] * scale * gain_ref[:, cut]).astype(BF16)

    def codes(s, ids):
        mb = s % 2
        named = [[ids[2 * mb + j, b] for j in range(2)] for b in range(blocks)]
        code = []
        for b in range(blocks):
            code.append([])
            for j in range(2):
                slot = jnp.int32(0)
                for earlier in range(b):
                    for other in range(2):
                        slot = slot + (named[earlier][other] == named[b][j]).astype(jnp.int32)
                code[b].append(2 * named[b][j] + slot)
        return named, code

    def set_picker(s, ids):
        _, code = codes(s, ids)
        row = lax.broadcasted_iota(jnp.int32, (half, rows), 0)
        column = lax.broadcasted_iota(jnp.int32, (half, rows), 1)
        same = (row % BR == column % BR).astype(F32)
        total = jnp.zeros((half, rows), F32)
        for j in range(2):
            wanted = jnp.zeros((half, rows), jnp.int32)
            for b in range(blocks):
                wanted = wanted + (column // BR == b).astype(jnp.int32) * code[b][j]
            total = total + (row // BR == wanted).astype(F32)
        picker[s] = (total * same).astype(BF16)

    def pick(s, k):
        source = normed if s < 2 else far_normed
        chosen = jnp.dot(picker[s], source[s % 2, k], preferred_element_type=F32)
        sending[s, k] = chosen.astype(BF16)
        own = pl.ds(pl.multiple_of(x * pick_rows, pick_rows), pick_rows)
        mine = pl.ds(pl.multiple_of(own_half + x * pick_rows, pick_rows), pick_rows)
        arrived[s, k, mine, :] = sending[s, k, own, :]
        for i in range(1, XN):
            x_forward(s, k, i).start()

    def relay(s, k):
        z_forward(s % 2, k).wait_recv()
        pick(s, k)

    def gates(s, ids):
        source = normed if s < 2 else far_normed
        mb = s % 2

        @pl.loop(0, blocks)
        def _(b):
            at = pl.ds(pl.multiple_of(b * BR, BR), BR)
            sums = [jnp.zeros((BR, LANES), F32) for _ in range(EXPERTS)]
            for k in range(CHUNKS):
                for t in range(tiles):
                    value = source[mb, k, at, t * LANES : (t + 1) * LANES].astype(F32)
                    first = k * width + t * LANES
                    for e in range(EXPERTS):
                        sums[e] = sums[e] + value * router_ref[e : e + 1, first : first + LANES]
            for e in range(EXPERTS):
                total = jnp.sum(sums[e], axis=-1, keepdims=True)
                scores[e, at, :] = jnp.broadcast_to(jax.nn.sigmoid(total), (BR, LANES))

        named, code = codes(s, ids)
        column = lax.broadcasted_iota(jnp.int32, (BR, LANES), 1)
        row = lax.broadcasted_iota(jnp.int32, (BR, LANES), 0)
        same = (column % BR == row).astype(F32)
        for b in range(blocks):
            at = slice(b * BR, (b + 1) * BR)
            score = []
            for j in range(2):
                value = jnp.zeros((BR, LANES), F32)
                for e in range(EXPERTS):
                    value = value + scores[e, at, :] * (named[b][j] == e).astype(F32)
                score.append(value)
            total = score[0] + score[1]
            for first in range(0, half, LANES):
                place = (column + first) // BR
                value = jnp.zeros((BR, LANES), F32)
                for j in range(2):
                    value = value + (place == code[b][j]).astype(F32) * same * (score[j] / total)
                main = value.astype(BF16)
                mixer[s, at, first : first + LANES] = main
                mixer_rest[s, at, first : first + LANES] = (value - main.astype(F32)).astype(BF16)

    def to_core(s, k):
        for i in range(1, XN):
            x_forward(s, k, i).wait_recv()
        core_forward(s, k).start()

    def experts(s):
        for k in range(CHUNKS):
            core_forward(s, k).wait_recv()
            core_forward(s, k).wait_send()

        @pl.loop(0, 2)
        def _(t):
            at = pl.ds(pl.multiple_of(t * half, half), half)
            gate_pre = jnp.zeros((half, units), F32)
            up_pre = jnp.zeros((half, units), F32)
            for k in range(CHUNKS):
                value = arrived[s, k, at, :]
                cut = slice(k * width, (k + 1) * width)
                gate_pre = gate_pre + jnp.dot(value, gate_w[cut, :], preferred_element_type=F32)
                up_pre = up_pre + jnp.dot(value, up_w[cut, :], preferred_element_type=F32)
            hidden[at, :] = (jax.nn.silu(gate_pre) * up_pre).astype(BF16)

        @pl.loop(0, CHUNKS)
        def _(k):
            for first in (mate_half, own_half):
                at = pl.ds(first, half)
                part = jnp.dot(hidden[at, :], down_w[k], preferred_element_type=F32)
                arrived[s, k, at, :] = part.astype(BF16)
                if first is mate_half:
                    core_part(s, k).start()

    def pair_sum(s, k):
        core_part(s, k).wait_recv()

        @pl.loop(0, XN)
        def _(i):
            at = pl.ds(pl.multiple_of(i * pick_rows, pick_rows), pick_rows)
            mine = pl.ds(pl.multiple_of(own_half + i * pick_rows, pick_rows), pick_rows)
            total = arrived[s, k, mine, :].astype(F32) + core_sum[s, k, at, :].astype(F32)
            arrived[s, k, mine, :] = total.astype(BF16)

        here = pl.ds(pl.multiple_of(x * pick_rows, pick_rows), pick_rows)
        mine = pl.ds(pl.multiple_of(own_half + x * pick_rows, pick_rows), pick_rows)
        returned[s, k, here, :] = arrived[s, k, mine, :]

    def send_back(s, k):
        for i in range(1, XN):
            x_return(s, k, i).start()

    def weighted(s, k):
        value = returned[s, k]
        return jnp.dot(mixer[s], value, preferred_element_type=F32) + jnp.dot(
            mixer_rest[s], value, preferred_element_type=F32
        )

    def combine(s, k):
        mb = s % 2
        for i in range(1, XN):
            x_return(s, k, i).wait_recv()
        z_out[mb, k] = weighted(s, k).astype(BF16)
        z_return(mb, k).start()

    def finish(mb, k):
        for i in range(1, XN):
            x_return(mb, k, i).wait_recv()
        z_return(mb, k).wait_recv()
        total = weighted(mb, k) + z_in[mb, k].astype(F32)
        mixed = acts[mb, :, k * width : (k + 1) * width].astype(F32) + ROUTE_SCALE * total
        finished[mb, k] = mixed.astype(BF16)
        shift(mb, k).start()

    act_copies = [
        pltpu.make_async_copy(source.at[0], acts.at[mb], act_sem.at[mb])
        for mb, source in enumerate((rise_hbm, fall_hbm))
    ]
    weight_copies = [
        pltpu.make_async_copy(gate_hbm.at[0], gate_w, w_sem.at[0]),
        pltpu.make_async_copy(up_hbm.at[0], up_w, w_sem.at[1]),
    ] + [
        pltpu.make_async_copy(down_hbm.at[0, :, pl.ds(k * width, width)], down_w.at[k], dw_sem.at[k])
        for k in range(CHUNKS)
    ]
    ids_copy = pltpu.make_async_copy(ids_hbm, ids_own, ids_sem.at[0])
    act_copies[0].start()
    ids_copy.start()
    act_copies[1].start()
    for copy in weight_copies:
        copy.start()

    barrier = pltpu.get_barrier_semaphore()
    partners = [(seg, x_device(i)) for i in range(1, XN)]
    partners += [(seg, z_mate), (seg, core_mate), (seg_up, me), (seg_down, me)]
    for partner in partners:
        pl.semaphore_signal(barrier, inc=1, device_id=partner, device_id_type=MESH)

    act_copies[0].wait()
    normalize(0)
    ids_copy.wait()
    set_picker(0, ids_own)
    pl.semaphore_wait(barrier, len(partners))

    every = range(CHUNKS)
    rise, fall, far_rise, far_fall = range(4)
    for k in every:
        z_forward(0, k).start()
    ids_exchange.start()
    for k in every:
        pick(rise, k)
    set_picker(fall, ids_own)
    act_copies[1].wait()
    normalize(1)
    for k in every:
        z_forward(1, k).start()
    gates(rise, ids_own)
    ids_exchange.wait()
    ids_far_copy = pltpu.make_async_copy(ids_land, ids_far, ids_sem.at[1])
    ids_far_copy.start()
    ids_far_copy.wait()
    set_picker(far_rise, ids_far)
    set_picker(far_fall, ids_far)
    to_core(rise, 0)
    relay(far_rise, 0)
    pick(fall, 0)
    for k in every[1:]:
        to_core(rise, k)
    for copy in weight_copies:
        copy.wait()
    experts(rise)
    for k in every[1:]:
        relay(far_rise, k)
        pick(fall, k)
    for k in every:
        pair_sum(rise, k)
    gates(fall, ids_own)
    for k in every:
        to_core(far_rise, k)
        to_core(fall, k)
    experts(far_rise)
    for k in every:
        pair_sum(far_rise, k)
        send_back(far_rise, k)
    gates(far_rise, ids_far)
    for k in every[: CHUNKS // 2]:
        relay(far_fall, k)
    experts(fall)
    for k in every:
        pair_sum(fall, k)
    for k in every[: CHUNKS // 2]:
        combine(far_rise, k)
    for k in every[CHUNKS // 2 :]:
        relay(far_fall, k)
        combine(far_rise, k)
    gates(far_fall, ids_far)
    for k in every[: CHUNKS // 2]:
        send_back(rise, k)
    for k in every:
        to_core(far_fall, k)
    experts(far_fall)
    for k in every:
        pair_sum(far_fall, k)
        send_back(far_fall, k)
    for k in every[CHUNKS // 2 :]:
        send_back(rise, k)
    for k in every:
        send_back(fall, k)
    for k in every[: CHUNKS // 2]:
        finish(0, k)
    for k in every:
        combine(far_fall, k)
    for k in every[CHUNKS // 2 :]:
        finish(0, k)
    for k in every:
        finish(1, k)

    for k in every:
        for mb in range(2):
            z_forward(mb, k).wait_send()
            z_return(mb, k).wait_send()
            shift(mb, k).wait_send()
        for s in range(4):
            core_part(s, k).wait_send()
            for i in range(1, XN):
                x_forward(s, k, i).wait_send()
                x_return(s, k, i).wait_send()
    for k in every:
        for mb in range(2):
            shift(mb, k).wait_recv()


def on_device(
    rising_acts,
    falling_acts,
    norm_gain,
    router_weight,
    gate_weight,
    up_weight,
    down_weight,
    rising_ids,
    falling_ids,
):
    rows, features = rising_acts.shape[1:]
    units = gate_weight.shape[2]
    width = features // CHUNKS
    half = XN * 2 * BR
    segments = lax.axis_size("segment")
    named = jnp.concatenate([rising_ids[0].T, falling_ids[0].T], axis=0)
    ids = jnp.pad(named, ((0, 8 - named.shape[0]), (0, LANES - named.shape[1])))
    dma = pltpu.SemaphoreType.DMA
    hbm = pl.BlockSpec(memory_space=pl.ANY)
    vmem = pl.BlockSpec(memory_space=pltpu.VMEM)
    result = jax.ShapeDtypeStruct(rising_acts.shape, BF16)
    return pl.pallas_call(
        functools.partial(relay_kernel, rows, features, units, segments),
        out_shape=(result, result),
        in_specs=[hbm, hbm, vmem, vmem, hbm, hbm, hbm, hbm],
        out_specs=(hbm, hbm),
        scratch_shapes=[
            pltpu.VMEM((2, rows, features), BF16),
            pltpu.VMEM((features, units), BF16),
            pltpu.VMEM((features, units), BF16),
            pltpu.VMEM((CHUNKS, units, width), BF16),
            pltpu.SMEM((8, LANES), jnp.int32),
            pltpu.VMEM((8, LANES), jnp.int32),
            pltpu.SMEM((8, LANES), jnp.int32),
            pltpu.VMEM((4, half, rows), BF16),
            pltpu.VMEM((4, rows, half), BF16),
            pltpu.VMEM((4, rows, half), BF16),
            pltpu.VMEM((2, CHUNKS, rows, width), BF16),
            pltpu.VMEM((2, CHUNKS, rows, width), BF16),
            pltpu.VMEM((4, CHUNKS, half, width), BF16),
            pltpu.VMEM((4, CHUNKS, 2 * half, width), BF16),
            pltpu.VMEM((2 * half, units), BF16),
            pltpu.VMEM((4, CHUNKS, half, width), BF16),
            pltpu.VMEM((4, CHUNKS, half, width), BF16),
            pltpu.VMEM((2, CHUNKS, rows, width), BF16),
            pltpu.VMEM((2, CHUNKS, rows, width), BF16),
            pltpu.VMEM((2, CHUNKS, rows, width), BF16),
            pltpu.VMEM((EXPERTS, rows, LANES), F32),
            dma((2,)),
            dma((2,)),
            dma((CHUNKS,)),
            dma((2,)),
            dma,
            dma,
            dma((2, CHUNKS)),
            dma((2, CHUNKS)),
            dma((4, CHUNKS, XN - 1)),
            dma((4, CHUNKS, XN - 1)),
            dma((4, CHUNKS)),
            dma((4, CHUNKS)),
            dma((4, CHUNKS)),
            dma((4, CHUNKS)),
            dma((4, CHUNKS, XN - 1)),
            dma((4, CHUNKS, XN - 1)),
            dma((2, CHUNKS)),
            dma((2, CHUNKS)),
            dma((2, CHUNKS)),
            dma((2, CHUNKS)),
        ],
        compiler_params=pltpu.CompilerParams(
            collective_id=0, has_side_effects=True, vmem_limit_bytes=60 << 20
        ),
        name="relay",
    )(
        rising_acts,
        falling_acts,
        norm_gain,
        router_weight[0].T,
        gate_weight,
        up_weight,
        down_weight,
        ids,
    )


def solution(mesh):
    return jax.shard_map(
        on_device,
        mesh=mesh,
        in_specs=(
            P("segment", "expert", None),
            P("segment", "expert", None),
            P("segment", None),
            P("segment", None, None),
            P("segment", None, "expert"),
            P("segment", None, "expert"),
            P("segment", "expert", None),
            P("segment", "expert", None),
            P("segment", "expert", None),
        ),
        out_specs=(P("segment", "expert", None), P("segment", "expert", None)),
        check_vma=False,
    )
```

time: 756 us -> 230 us (0.30)
  waiting for transfers between devices: 531 us -> 0 us
  Pallas kernels: 0 us -> 221 us
  starting transfers between devices: 126 us -> 0 us
  matrix products: 59.5 us -> 0 us
  other arithmetic: 18 us -> 0.7 us
  local copies, waits for them, and re-layouts: 15.9 us -> 3.77 us
    all_to_all x4 -> x0, waiting for transfers between devices: 406 us -> none  [the longest x2 228 us: moe_layer(): lax.all_to_all(outgoing, 'expert', split_axis=0, concat_axis=0, tiled=True)]
    pallas_call x0 -> x1, Pallas kernels: none -> 221 us  [on_device(): pl.pallas_call(functools.partial(relay_kernel, rows, features, units, seg...]
    ppermute x2 -> x0, waiting for transfers between devices: 125 us -> none  [from_behind(): return lax.ppermute(value, axis, pairs)]
    ppermute x2 -> x0, starting transfers between devices: 93.1 us -> none  [from_behind(): return lax.ppermute(value, axis, pairs)]
    dot_general x10 -> x0, matrix products: 59.5 us -> none  [the longest x2 30.5 us: moe_layer(): jnp.dot(hidden, down_slab, preferred_element_type=jnp.float32)]
    all_to_all x4 -> x0, starting transfers between devices: 33.2 us -> none  [the longest x2 19.3 us: moe_layer(): lax.all_to_all(outgoing, 'expert', split_axis=0, concat_axis=0, tiled=True)]
    convert_element_type x10 -> x0, other arithmetic: 12.7 us -> none  [the longest x2 8.49 us: pair_levels(): (stacked[:, 0::2].astype(jnp.float32) + stacked[:, 1::2].astype(jnp.float...]
    broadcast_in_dim x2 -> x0, local copies, waits for them, and re-layouts: 9.09 us -> none  [moe_layer(): outgoing = jnp.repeat(picked, group_size, axis=0)]
  transfers between devices with their start and end apart: 6 -> 0, of which waited for: 6 -> 0; matrix products, arithmetic and copies ran while one was open for 10% -> 0% of each run, Pallas kernels for 0% -> 0%
where the time goes in v1:
time: 230 us; the launch traced here: 226 us
  Pallas kernels  221 us (96%)
  local copies, waits for them, and re-layouts  3.77 us (2%)
    pallas_call x1, Pallas kernels, on_device(): pl.pallas_call(functools.partial(relay_kernel, rows, features, units, seg...  221 us

profile of v1, /device:TPU:1, one launch (start us, length us, event | category | flops | bytes accessed | tf_op | source)
XLA Modules:
  0.0 226.3 jit_solution(2855758105949859402)
XLA Ops:
  0.6 0.7 pad_add_fusion
  1.3 0.6 pad.4.ids_hbm
  1.9 221.2 %relay.1 = (bf16[1,128,3584]{2,1,0:T(8,128)(2,1)}, bf16[1,128,3584]{2,1,0:T(8,128)(2,1)}) custom-call(bf16[1,128,3584]{2,1,0:T(8,128)(2,1)} %rise_hbm.1, bf16[1,128,3584]{2,1,0:T(8,128)(2,1)} %fall_hbm.1, f32[1,3584]{1,0:T(1,128)} %gain_ref.1, f32[4,3584]{1,0:T(4,128)} %bitcast.9, bf16[1,3584,256]{2,1,0:T(8,128)(2,1)} %gate_hbm.1, ...), custom_call_target="tpu_custom_call" | custom-call | tf_op jit(solution)/shard_map/relay/pallas_call | solution.py:485
  223.1 0.0 copy-start
  223.1 2.2 copy.13
  225.3 0.0 copy-done
  225.4 0.9 copy.14
Async XLA Ops:
  223.1 2.3 copy-start

commit v2 on v1

--- a/solution.py
+++ b/solution.py
@@ -12,7 +12,10 @@
 ROUTE_SCALE = 2.5
 EXPERTS = 4
 XN = 4
-CHUNKS = 4
+CHUNKS = 7
+FILL = (2, 5)
+YN = 4
+DETOURS = ((1, 2, 0, 1, 2), (2, 1, 3, 2, 1))
 BR = 32
 LANES = 128
 F32 = jnp.float32
@@ -75,6 +78,9 @@
     zr_rs,
     y_ss,
     y_rs,
+    passing,
+    pass_ss,
+    pass_rs,
 ):
     width = features // CHUNKS
     pick_rows = 2 * BR
@@ -91,6 +97,14 @@
     core_mate = me + 1 - 2 * core
     seg_up = lax.rem(seg + 1, segments)
     seg_down = lax.rem(seg + segments - 1, segments)
+    y = lax.rem(seg, YN)
+    z_lo = seg // YN
+    z_count = segments // YN
+    seg_base = seg - y
+    base_up = lax.rem(z_lo + 1, z_count) * YN
+    base_down = lax.rem(z_lo + z_count - 1, z_count) * YN
+    at_edge = (y == YN - 1, y == 0)
+    past_edge = (base_up, base_down + YN - 1)
     own_half = pl.multiple_of(core * half, half)
     mate_half = pl.multiple_of((1 - core) * half, half)
 
@@ -168,6 +182,27 @@
             send_sem=y_ss.at[mb, k],
             recv_sem=y_rs.at[mb, k],
             device_id=(seg_up if mb == 0 else seg_down, me),
+            device_id_type=MESH,
+        )
+
+    def detour(mb, k):
+        return pltpu.make_async_remote_copy(
+            src_ref=finished.at[mb, k],
+            dst_ref=passing.at[mb, k],
+            send_sem=y_ss.at[mb, k],
+            recv_sem=pass_rs.at[mb, k],
+            device_id=(seg_base + DETOURS[mb][k], me),
+            device_id_type=MESH,
+        )
+
+    def onward(mb, k):
+        out = rise_out if mb == 0 else fall_out
+        return pltpu.make_async_remote_copy(
+            src_ref=passing.at[mb, k],
+            dst_ref=out.at[0, :, pl.ds(k * width, width)],
+            send_sem=pass_ss.at[mb, k],
+            recv_sem=y_rs.at[mb, k],
+            device_id=(past_edge[mb], me),
             device_id_type=MESH,
         )
 
@@ -340,7 +375,27 @@
         total = weighted(mb, k) + z_in[mb, k].astype(F32)
         mixed = acts[mb, :, k * width : (k + 1) * width].astype(F32) + ROUTE_SCALE * total
         finished[mb, k] = mixed.astype(BF16)
-        shift(mb, k).start()
+        if k < len(DETOURS[mb]):
+
+            @pl.when(at_edge[mb])
+            def _():
+                detour(mb, k).start()
+
+            @pl.when(jnp.logical_not(at_edge[mb]))
+            def _():
+                shift(mb, k).start()
+
+        else:
+            shift(mb, k).start()
+
+    def pass_on(mb, k):
+        if k >= len(DETOURS[mb]):
+            return
+
+        @pl.when(y == DETOURS[mb][k])
+        def _():
+            detour(mb, k).wait_recv()
+            onward(mb, k).start()
 
     act_copies = [
         pltpu.make_async_copy(source.at[0], acts.at[mb], act_sem.at[mb])
@@ -357,26 +412,43 @@
     act_copies[0].start()
     ids_copy.start()
     act_copies[1].start()
+
+    barrier = pltpu.get_barrier_semaphore()
+    partners = [(seg, x_device(i)) for i in range(1, XN)]
+    partners += [(seg, z_mate), (seg, core_mate), (base_up, me), (base_down + YN - 1, me)]
+    partners += [(seg_base + lax.rem(y + j, YN), me) for j in range(1, YN)]
+
+    def greet(partner):
+        pl.semaphore_signal(barrier, inc=1, device_id=partner, device_id_type=MESH)
+
+    for partner in partners:
+        greet(partner)
+
+    @pl.when(at_edge[1])
+    def _():
+        for j in range(YN - 1):
+            greet((base_down + j, me))
+
+    @pl.when(at_edge[0])
+    def _():
+        for j in range(1, YN):
+            greet((base_up + j, me))
+
+    at_either = jnp.logical_or(at_edge[0], at_edge[1]).astype(jnp.int32)
+
+    act_copies[0].wait()
+    normalize(0)
     for copy in weight_copies:
         copy.start()
-
-    barrier = pltpu.get_barrier_semaphore()
-    partners = [(seg, x_device(i)) for i in range(1, XN)]
-    partners += [(seg, z_mate), (seg, core_mate), (seg_up, me), (seg_down, me)]
-    for partner in partners:
-        pl.semaphore_signal(barrier, inc=1, device_id=partner, device_id_type=MESH)
-
-    act_copies[0].wait()
-    normalize(0)
     ids_copy.wait()
     set_picker(0, ids_own)
-    pl.semaphore_wait(barrier, len(partners))
+    pl.semaphore_wait(barrier, len(partners) + (YN - 1) * at_either)
 
     every = range(CHUNKS)
     rise, fall, far_rise, far_fall = range(4)
+    ids_exchange.start()
     for k in every:
         z_forward(0, k).start()
-    ids_exchange.start()
     for k in every:
         pick(rise, k)
     set_picker(fall, ids_own)
@@ -398,16 +470,20 @@
         to_core(rise, k)
     for copy in weight_copies:
         copy.wait()
+    pick(fall, 1)
     experts(rise)
     for k in every[1:]:
         relay(far_rise, k)
-        pick(fall, k)
+        if k + 1 < CHUNKS:
+            pick(fall, k + 1)
     for k in every:
         pair_sum(rise, k)
     gates(fall, ids_own)
     for k in every:
         to_core(far_rise, k)
         to_core(fall, k)
+    for k in every[: FILL[0]]:
+        send_back(rise, k)
     experts(far_rise)
     for k in every:
         pair_sum(far_rise, k)
@@ -424,7 +500,7 @@
         relay(far_fall, k)
         combine(far_rise, k)
     gates(far_fall, ids_far)
-    for k in every[: CHUNKS // 2]:
+    for k in every[FILL[0] : FILL[1]]:
         send_back(rise, k)
     for k in every:
         to_core(far_fall, k)
@@ -432,18 +508,24 @@
     for k in every:
         pair_sum(far_fall, k)
         send_back(far_fall, k)
-    for k in every[CHUNKS // 2 :]:
+    for k in every[FILL[1] :]:
         send_back(rise, k)
     for k in every:
         send_back(fall, k)
-    for k in every[: CHUNKS // 2]:
+    early = max(FILL[1] - 1, 1)
+    for k in every[:early]:
         finish(0, k)
     for k in every:
         combine(far_fall, k)
-    for k in every[CHUNKS // 2 :]:
-        finish(0, k)
-    for k in every:
-        finish(1, k)
+        if k < early:
+            pass_on(0, k)
+    last = [(0, k) for k in every[early:]] + [(1, k) for k in every]
+    for i, step in enumerate(last):
+        finish(*step)
+        if i >= 2:
+            pass_on(*last[i - 2])
+    for step in last[-2:]:
+        pass_on(*step)
 
     for k in every:
         for mb in range(2):
@@ -455,6 +537,13 @@
             for i in range(1, XN):
                 x_forward(s, k, i).wait_send()
                 x_return(s, k, i).wait_send()
+    for mb in range(2):
+        for k, by in enumerate(DETOURS[mb]):
+
+            @pl.when(y == by)
+            def _():
+                onward(mb, k).wait_send()
+
     for k in every:
         for mb in range(2):
             shift(mb, k).wait_recv()
@@ -529,6 +618,9 @@
             dma((2, CHUNKS)),
             dma((2, CHUNKS)),
             dma((2, CHUNKS)),
+            pltpu.VMEM((2, len(DETOURS[0]), rows, width), BF16),
+            dma((2, CHUNKS)),
+            dma((2, CHUNKS)),
         ],
         compiler_params=pltpu.CompilerParams(
             collective_id=0, has_side_effects=True, vmem_limit_bytes=60 << 20

time: 230 us -> 203 us (0.88); the launches traced: 226 us -> 203 us
  Pallas kernels: 221 us -> 197 us
    pallas_call x1, Pallas kernels: 221 us -> 197 us  [on_device(): pl.pallas_call(functools.partial(relay_kernel, rows, features, units, seg...]
where the time goes in v2:
time: 203 us
  Pallas kernels  197 us (97%)
  local copies, waits for them, and re-layouts  3.77 us (2%)
    pallas_call x1, Pallas kernels, on_device(): pl.pallas_call(functools.partial(relay_kernel, rows, features, units, seg...  197 us

profile of v2, /device:TPU:1, one launch (start us, length us, event | category | flops | bytes accessed | tf_op | source)
XLA Modules:
  0.0 202.6 jit_solution(13106020270884035759)
XLA Ops:
  0.6 0.7 pad_add_fusion
  1.3 0.6 pad.4.ids_hbm
  1.9 197.5 %relay.1 = (bf16[1,128,3584]{2,1,0:T(8,128)(2,1)}, bf16[1,128,3584]{2,1,0:T(8,128)(2,1)}) custom-call(bf16[1,128,3584]{2,1,0:T(8,128)(2,1)} %rise_hbm.1, bf16[1,128,3584]{2,1,0:T(8,128)(2,1)} %fall_hbm.1, f32[1,3584]{1,0:T(1,128)} %gain_ref.1, f32[4,3584]{1,0:T(4,128)} %bitcast.9, bf16[1,3584,256]{2,1,0:T(8,128)(2,1)} %gate_hbm.1, ...), custom_call_target="tpu_custom_call" | custom-call | tf_op jit(solution)/shard_map/relay/pallas_call | solution.py:574
  199.4 0.0 copy-start
  199.4 2.2 %copy.13 = bf16[1,128,3584]{2,1,0:T(8,128)(2,1)} copy(bf16[1,128,3584]{2,1,0:T(8,128)(2,1)} %get-tuple-element.4) | data formatting | bytes 1835008
  201.7 0.0 copy-done
  201.7 0.9 copy.14
Async XLA Ops:
  199.4 2.3 %copy-start = (bf16[1,128,3584]{2,1,0:T(8,128)(2,1)S(1)}, bf16[1,128,3584]{2,1,0:T(8,128)(2,1)}, u32[]{:S(2)}) copy-start(bf16[1,128,3584]{2,1,0:T(8,128)(2,1)} %get-tuple-element.5) | copy-start | bytes 2752516

commit v3 on v2

--- a/solution.py
+++ b/solution.py
@@ -15,7 +15,7 @@
 CHUNKS = 7
 FILL = (2, 5)
 YN = 4
-DETOURS = ((1, 2, 0, 1, 2), (2, 1, 3, 2, 1))
+DETOURS = ((1, 2, 0, 1, 2), (2, 1, 3, 2))
 BR = 32
 LANES = 128
 F32 = jnp.float32
@@ -34,16 +34,19 @@
     gate_hbm,
     up_hbm,
     down_hbm,
-    ids_hbm,
+    rise_ids,
+    fall_ids,
     rise_out,
     fall_out,
     acts,
     gate_w,
     up_w,
     down_w,
-    ids_own,
     ids_land,
-    ids_far,
+    ids_rise,
+    ids_fall,
+    far_rise_ids,
+    far_fall_ids,
     picker,
     mixer,
     mixer_rest,
@@ -206,14 +209,17 @@
             device_id_type=MESH,
         )
 
-    ids_exchange = pltpu.make_async_remote_copy(
-        src_ref=ids_hbm,
-        dst_ref=ids_land,
-        send_sem=ids_ss,
-        recv_sem=ids_rs,
-        device_id=(seg, z_mate),
-        device_id_type=MESH,
-    )
+    ids_exchange = [
+        pltpu.make_async_remote_copy(
+            src_ref=source,
+            dst_ref=ids_land.at[mb],
+            send_sem=ids_ss.at[mb],
+            recv_sem=ids_rs.at[mb],
+            device_id=(seg, z_mate),
+            device_id_type=MESH,
+        )
+        for mb, source in enumerate((rise_ids, fall_ids))
+    ]
 
     def normalize(mb):
         @pl.loop(0, blocks)
@@ -227,7 +233,7 @@
 
     def codes(s, ids):
         mb = s % 2
-        named = [[ids[2 * mb + j, b] for j in range(2)] for b in range(blocks)]
+        named = [[ids[mb][j, b] for j in range(2)] for b in range(blocks)]
         code = []
         for b in range(blocks):
             code.append([])
@@ -408,9 +414,18 @@
         pltpu.make_async_copy(down_hbm.at[0, :, pl.ds(k * width, width)], down_w.at[k], dw_sem.at[k])
         for k in range(CHUNKS)
     ]
-    ids_copy = pltpu.make_async_copy(ids_hbm, ids_own, ids_sem.at[0])
+    ids_own = (ids_rise, ids_fall)
+    ids_far = (far_rise_ids, far_fall_ids)
+    ids_copies = [
+        pltpu.make_async_copy(source, ids_own[mb], ids_sem.at[mb])
+        for mb, source in enumerate((rise_ids, fall_ids))
+    ]
+    ids_far_copies = [
+        pltpu.make_async_copy(ids_land.at[mb], ids_far[mb], ids_sem.at[2 + mb]) for mb in range(2)
+    ]
     act_copies[0].start()
-    ids_copy.start()
+    for copy in ids_copies:
+        copy.start()
     act_copies[1].start()
 
     barrier = pltpu.get_barrier_semaphore()
@@ -440,13 +455,15 @@
     normalize(0)
     for copy in weight_copies:
         copy.start()
-    ids_copy.wait()
+    for copy in ids_copies:
+        copy.wait()
     set_picker(0, ids_own)
     pl.semaphore_wait(barrier, len(partners) + (YN - 1) * at_either)
 
     every = range(CHUNKS)
     rise, fall, far_rise, far_fall = range(4)
-    ids_exchange.start()
+    for copy in ids_exchange:
+        copy.start()
     for k in every:
         z_forward(0, k).start()
     for k in every:
@@ -457,10 +474,12 @@
     for k in every:
         z_forward(1, k).start()
     gates(rise, ids_own)
-    ids_exchange.wait()
-    ids_far_copy = pltpu.make_async_copy(ids_land, ids_far, ids_sem.at[1])
-    ids_far_copy.start()
-    ids_far_copy.wait()
+    for copy in ids_exchange:
+        copy.wait()
+    for copy in ids_far_copies:
+        copy.start()
+    for copy in ids_far_copies:
+        copy.wait()
     set_picker(far_rise, ids_far)
     set_picker(far_fall, ids_far)
     to_core(rise, 0)
@@ -504,28 +523,39 @@
         send_back(rise, k)
     for k in every:
         to_core(far_fall, k)
+        if 1 <= k <= FILL[0]:
+            finish(0, k - 1)
+    for k in every[: FILL[0]]:
+        pass_on(0, k)
     experts(far_fall)
     for k in every:
         pair_sum(far_fall, k)
         send_back(far_fall, k)
-    for k in every[FILL[1] :]:
-        send_back(rise, k)
+    late = list(every[FILL[1] :])
     for k in every:
         send_back(fall, k)
-    early = max(FILL[1] - 1, 1)
-    for k in every[:early]:
+        if k < len(late):
+            send_back(rise, late[k])
+    for k in every[FILL[0] : FILL[1]]:
         finish(0, k)
     for k in every:
         combine(far_fall, k)
-        if k < early:
+        if FILL[0] <= k < FILL[1]:
             pass_on(0, k)
-    last = [(0, k) for k in every[early:]] + [(1, k) for k in every]
-    for i, step in enumerate(last):
-        finish(*step)
-        if i >= 2:
-            pass_on(*last[i - 2])
-    for step in last[-2:]:
-        pass_on(*step)
+    last = []
+    for k in every:
+        last.append((1, k))
+        if k < len(late):
+            last.append((0, late[k]))
+    waiting = []
+    for mb, k in last:
+        finish(mb, k)
+        while waiting and waiting[0][2] <= 1:
+            pass_on(*waiting.pop(0)[:2])
+        waiting = [(*step, lag - 1) for *step, lag in waiting]
+        waiting.append((mb, k, 1 if mb == 1 and k >= 2 else 2))
+    for mb, k, _ in waiting:
+        pass_on(mb, k)
 
     for k in every:
         for mb in range(2):
@@ -565,8 +595,7 @@
     width = features // CHUNKS
     half = XN * 2 * BR
     segments = lax.axis_size("segment")
-    named = jnp.concatenate([rising_ids[0].T, falling_ids[0].T], axis=0)
-    ids = jnp.pad(named, ((0, 8 - named.shape[0]), (0, LANES - named.shape[1])))
+    top, blocks = rising_ids.shape[2], rising_ids.shape[1]
     dma = pltpu.SemaphoreType.DMA
     hbm = pl.BlockSpec(memory_space=pl.ANY)
     vmem = pl.BlockSpec(memory_space=pltpu.VMEM)
@@ -574,16 +603,17 @@
     return pl.pallas_call(
         functools.partial(relay_kernel, rows, features, units, segments),
         out_shape=(result, result),
-        in_specs=[hbm, hbm, vmem, vmem, hbm, hbm, hbm, hbm],
+        in_specs=[hbm, hbm, vmem, vmem, hbm, hbm, hbm, hbm, hbm],
         out_specs=(hbm, hbm),
         scratch_shapes=[
             pltpu.VMEM((2, rows, features), BF16),
             pltpu.VMEM((features, units), BF16),
             pltpu.VMEM((features, units), BF16),
             pltpu.VMEM((CHUNKS, units, width), BF16),
-            pltpu.SMEM((8, LANES), jnp.int32),
-            pltpu.VMEM((8, LANES), jnp.int32),
-            pltpu.SMEM((8, LANES), jnp.int32),
+            pltpu.VMEM((2, top, blocks), jnp.int32),
+        ]
+        + [pltpu.SMEM((top, blocks), jnp.int32)] * 4
+        + [
             pltpu.VMEM((4, half, rows), BF16),
             pltpu.VMEM((4, rows, half), BF16),
             pltpu.VMEM((4, rows, half), BF16),
@@ -601,9 +631,9 @@
             dma((2,)),
             dma((2,)),
             dma((CHUNKS,)),
+            dma((4,)),
             dma((2,)),
-            dma,
-            dma,
+            dma((2,)),
             dma((2, CHUNKS)),
             dma((2, CHUNKS)),
             dma((4, CHUNKS, XN - 1)),
@@ -634,7 +664,8 @@
         gate_weight,
         up_weight,
         down_weight,
-        ids,
+        rising_ids[0].T,
+        falling_ids[0].T,
     )
 
 

time: 203 us -> 198 us (0.975)
  Pallas kernels: 197 us -> 194 us
    pallas_call x1, Pallas kernels: 197 us -> 194 us  [on_device(): pl.pallas_call(functools.partial(relay_kernel, rows, features, units, seg...]
where the time goes in v3:
time: 198 us
  Pallas kernels  194 us (98%)
  local copies, waits for them, and re-layouts  3.17 us (2%)
    pallas_call x1, Pallas kernels, on_device(): pl.pallas_call(functools.partial(relay_kernel, rows, features, units, seg...  194 us

profile of v3, /device:TPU:1, one launch (start us, length us, event | category | flops | bytes accessed | tf_op | source)
XLA Modules:
  0.0 197.8 jit_solution(3207364144800075609)
XLA Ops:
  0.6 194.0 %relay.1 = (bf16[1,128,3584]{2,1,0:T(8,128)(2,1)}, bf16[1,128,3584]{2,1,0:T(8,128)(2,1)}) custom-call(bf16[1,128,3584]{2,1,0:T(8,128)(2,1)} %rise_hbm.1, bf16[1,128,3584]{2,1,0:T(8,128)(2,1)} %fall_hbm.1, f32[1,3584]{1,0:T(1,128)} %gain_ref.1, f32[4,3584]{1,0:T(4,128)} %bitcast.9, bf16[1,3584,256]{2,1,0:T(8,128)(2,1)} %gate_hbm.1, ...), custom_call_target="tpu_custom_call" | custom-call | tf_op jit(solution)/shard_map/relay/pallas_call | solution.py:603
  194.7 0.0 copy-start
  194.7 2.2 %copy.13 = bf16[1,128,3584]{2,1,0:T(8,128)(2,1)} copy(bf16[1,128,3584]{2,1,0:T(8,128)(2,1)} %get-tuple-element.4) | data formatting | bytes 1835008
  196.9 0.0 copy-done
  196.9 0.9 copy.14
Async XLA Ops:
  194.7 2.3 %copy-start = (bf16[1,128,3584]{2,1,0:T(8,128)(2,1)S(1)}, bf16[1,128,3584]{2,1,0:T(8,128)(2,1)}, u32[]{:S(2)}) copy-start(bf16[1,128,3584]{2,1,0:T(8,128)(2,1)} %get-tuple-element.5) | copy-start | bytes 2752516

commit v4 on v3

--- a/solution.py
+++ b/solution.py
@@ -12,6 +12,7 @@
 ROUTE_SCALE = 2.5
 EXPERTS = 4
 XN = 4
+FAR_FIRST = (2, 1, 3)
 CHUNKS = 7
 FILL = (2, 5)
 YN = 4
@@ -265,7 +266,7 @@
         own = pl.ds(pl.multiple_of(x * pick_rows, pick_rows), pick_rows)
         mine = pl.ds(pl.multiple_of(own_half + x * pick_rows, pick_rows), pick_rows)
         arrived[s, k, mine, :] = sending[s, k, own, :]
-        for i in range(1, XN):
+        for i in FAR_FIRST:
             x_forward(s, k, i).start()
 
     def relay(s, k):
@@ -358,7 +359,7 @@
         returned[s, k, here, :] = arrived[s, k, mine, :]
 
     def send_back(s, k):
-        for i in range(1, XN):
+        for i in FAR_FIRST:
             x_return(s, k, i).start()
 
     def weighted(s, k):

time: 198 us -> 198 us (level)
  no operation moved by 1% of the time
where the time goes in v4:
time: 198 us; the launch traced here: 197 us
  Pallas kernels  193 us (97%)
  local copies, waits for them, and re-layouts  3.17 us (2%)
    pallas_call x1, Pallas kernels, on_device(): pl.pallas_call(functools.partial(relay_kernel, rows, features, units, seg...  193 us

profile of v4, /device:TPU:1, one launch (start us, length us, event | category | flops | bytes accessed | tf_op | source)
XLA Modules:
  0.0 197.1 jit_solution(1212988147749743469)
XLA Ops:
  0.6 193.2 %relay.1 = (bf16[1,128,3584]{2,1,0:T(8,128)(2,1)}, bf16[1,128,3584]{2,1,0:T(8,128)(2,1)}) custom-call(bf16[1,128,3584]{2,1,0:T(8,128)(2,1)} %rise_hbm.1, bf16[1,128,3584]{2,1,0:T(8,128)(2,1)} %fall_hbm.1, f32[1,3584]{1,0:T(1,128)} %gain_ref.1, f32[4,3584]{1,0:T(4,128)} %bitcast.9, bf16[1,3584,256]{2,1,0:T(8,128)(2,1)} %gate_hbm.1, ...), custom_call_target="tpu_custom_call" | custom-call | tf_op jit(solution)/shard_map/relay/pallas_call | solution.py:604
  193.9 0.0 copy-start
  193.9 2.2 %copy.13 = bf16[1,128,3584]{2,1,0:T(8,128)(2,1)} copy(bf16[1,128,3584]{2,1,0:T(8,128)(2,1)} %get-tuple-element.4) | data formatting | bytes 1835008
  196.1 0.0 copy-done
  196.1 0.9 copy.14
Async XLA Ops:
  193.9 2.3 %copy-start = (bf16[1,128,3584]{2,1,0:T(8,128)(2,1)S(1)}, bf16[1,128,3584]{2,1,0:T(8,128)(2,1)}, u32[]{:S(2)}) copy-start(bf16[1,128,3584]{2,1,0:T(8,128)(2,1)} %get-tuple-element.5) | copy-start | bytes 2752516
